TPU v7x, 256 devices: a whole 4x4x8 slice. The times are simulated.
256 devices in a mesh: ctx: 32 (over y, z), tp: 8 (over x, core).
Axes of the slice: x: 4, y: 4, z: 8, core: 2. Of those that a mesh axis runs over, the one named last changes fastest.
Arguments:
- queries: bfloat16 [16384, 8192], P('ctx', 'tp'), may hold values from -6 to 6
- keys: bfloat16 [16384, 8192], P('ctx', 'tp'), may hold values from -6 to 6
- values: bfloat16 [16384, 8192], P('ctx', 'tp'), may hold values from -75 to 75
- gate: bfloat16 [16384, 8192], P('ctx', 'tp'), may hold values from -6 to 6
- gain: float32 [8192], P('tp'), may hold values from 0.1 to 1.9
- out_grad: bfloat16 [16384, 8192], P('ctx', 'tp'), may hold values from -6 to 6
Outputs:
- output: bfloat16 [16384, 8192], P('ctx', 'tp')
- query_grad: bfloat16 [16384, 8192], P('ctx', 'tp')
- key_grad: bfloat16 [16384, 8192], P('ctx', 'tp')
- value_grad: bfloat16 [16384, 8192], P('ctx', 'tp')
- gate_grad: bfloat16 [16384, 8192], P('ctx', 'tp')
All inputs are finite; a program needn't handle non-finite values.
Results may differ from a plain program's by a relative error of at most 0.005.
Values sent between devices are 32-bit elements; how exact they have to be, the bound alone decides.
No kernel may reach another device: no remote copies, remote signals or barrier semaphores. Data moves between devices by JAX's collectives and lax.ppermute only.
A program may use at most 128 MiB of HBM per device.

v0:
```python
import jax
import jax.numpy as jnp
from jax import lax
from jax.sharding import PartitionSpec as P

HD = 128
BLOCK = 512
D = 8192
EPS = 1e-06


def carried_in(value, axis, join, neutral, backward):
    count, mine = (lax.axis_size(axis), lax.axis_index(axis))
    pieces = lax.all_gather(value, axis)
    if backward:
        pieces = pieces[::-1]
        mine = count - 1 - mine
    running = jnp.full_like(value, 0) + jnp.asarray(neutral, value.dtype)

    def turn(position, running):
        longer = join(running, pieces[position])
        return jnp.where(position < mine, longer, running)

    return lax.fori_loop(0, count - 1, turn, running)


def add_states(earlier, later):
    return earlier + later


def local(queries, keys, values, gate, gain, out_grad):
    tok_rows, width = queries.shape
    heads_here = width // HD
    nblocks = tok_rows // BLOCK
    high = lax.Precision.HIGHEST

    def split(x):
        return x.reshape(nblocks, BLOCK, heads_here, HD)

    q_blocks, k_blocks, v_blocks = (split(queries), split(keys), split(values))
    row_ids = lax.broadcasted_iota(jnp.int32, (BLOCK, BLOCK), 0)
    col_ids = lax.broadcasted_iota(jnp.int32, (BLOCK, BLOCK), 1)
    causal = col_ids <= row_ids
    scores = jnp.einsum("nbhe,nche->nhbc", q_blocks, k_blocks, preferred_element_type=jnp.float32)
    attn = jnp.where(causal, scores, 0.0).astype(jnp.bfloat16)
    block_kv = jnp.einsum("nche,nchf->nhef", k_blocks, v_blocks, preferred_element_type=jnp.float32)
    device_kv = jnp.sum(block_kv, 0)
    local_before = jnp.cumsum(block_kv, 0) - block_kv
    empty = jnp.zeros_like(device_kv)
    carried = carried_in(device_kv, "ctx", add_states, empty, False)
    states = carried[None] + local_before
    inter = jnp.einsum("nbhe,nhef->nbhf", q_blocks.astype(jnp.float32), states, precision=high)
    intra = jnp.einsum("nhbc,nchf->nbhf", attn, v_blocks, preferred_element_type=jnp.float32)
    mixed = (intra + inter).reshape(tok_rows, width)
    sig = jax.nn.sigmoid(gate.astype(jnp.float32))
    dy_full = out_grad.astype(jnp.float32)
    dn = dy_full * gain * sig
    own_square = jnp.sum(mixed * mixed, axis=1)
    square_total = lax.psum(own_square, "tp")
    inv_rms = lax.rsqrt(square_total / D + EPS)[:, None]
    normed = mixed * inv_rms
    output = (normed * gain * sig).astype(jnp.bfloat16)
    cross_total = lax.psum(jnp.sum(dn * mixed, axis=1), "tp")
    project = inv_rms * (cross_total / D)[:, None]
    mixed_grad = (inv_rms * (dn - normed * project)).astype(jnp.bfloat16)
    gate_grad = (dy_full * gain * normed * sig * (1.0 - sig)).astype(jnp.bfloat16)
    d_blocks = split(mixed_grad)
    prob = jnp.where(
        causal,
        jnp.einsum("nbhf,nchf->nhbc", d_blocks, v_blocks, preferred_element_type=jnp.float32),
        0.0,
    ).astype(jnp.bfloat16)
    q_grad = jnp.einsum("nhbc,nche->nbhe", prob, k_blocks, preferred_element_type=jnp.float32)
    q_grad = q_grad + jnp.einsum(
        "nbhf,nhef->nbhe", d_blocks.astype(jnp.float32), states, precision=high
    )
    block_g = jnp.einsum("nbhe,nbhf->nhef", q_blocks, d_blocks, preferred_element_type=jnp.float32)
    local_after = jnp.flip(jnp.cumsum(jnp.flip(block_g, 0), 0), 0) - block_g
    device_g = jnp.sum(block_g, 0)
    later = carried_in(device_g, "ctx", add_states, empty, True)
    after = later[None] + local_after
    k_grad = jnp.einsum("nhbc,nbhe->nche", prob, q_blocks, preferred_element_type=jnp.float32)
    k_grad = k_grad + jnp.einsum(
        "nchf,nhef->nche", v_blocks.astype(jnp.float32), after, precision=high
    )
    v_grad = jnp.einsum("nhbc,nbhf->nchf", attn, d_blocks, preferred_element_type=jnp.float32)
    v_grad = v_grad + jnp.einsum(
        "nche,nhef->nchf", k_blocks.astype(jnp.float32), after, precision=high
    )
    return (
        output,
        q_grad.reshape(tok_rows, width).astype(jnp.bfloat16),
        k_grad.reshape(tok_rows, width).astype(jnp.bfloat16),
        v_grad.reshape(tok_rows, width).astype(jnp.bfloat16),
        gate_grad,
    )


def solution(mesh):
    return jax.shard_map(
        local,
        mesh=mesh,
        in_specs=(
            P("ctx", "tp"),
            P("ctx", "tp"),
            P("ctx", "tp"),
            P("ctx", "tp"),
            P("tp"),
            P("ctx", "tp"),
        ),
        out_specs=(P("ctx", "tp"), P("ctx", "tp"), P("ctx", "tp"), P("ctx", "tp"), P("ctx", "tp")),
        check_vma=False,
    )
```

profile of v0, /device:TPU:1, one launch (start us, length us, event | category | flops | bytes accessed | tf_op | source)
XLA Modules:
  0.0 434.1 jit_solution(13185674936705253317)
XLA Ops:
  7.2 2.6 copy.67
  9.8 1.6 copy.39
  11.4 2.9 fusion.9
  14.5 2.6 select_convert_fusion.1
  17.1 2.1 copy-done.1
  19.2 2.8 fusion.4
  22.0 136.4 %all-gather.5.cloned.1.call-done = f32[256,128,128]{2,1,0:T(8,128)} async-done(((f32[8,128,128]{2,1,0:T(8,128)}), f32[256,128,128]{2,1,0:T(8,128)}) %all-gather.5.cloned.1.call-update) | async-done | bytes 16777232 | tf_op jit(solution)/shard_map/all_gather | solution.py:14
  158.5 38.8 %while.28 = (s32[]{:T(128)}, f32[8,128,128]{2,1,0:T(8,128)S(1)}, s32[]{:T(128)}, f32[32,8,128,128]{3,2,1,0:T(8,128)}, s32[]{:T(128)}, /*index=5*/s32[]{:T(128)}) while((s32[]{:T(128)}, f32[8,128,128]{2,1,0:T(8,128)S(1)}, s32[]{:T(128)}, f32[32,8,128,128]{3,2,1,0:T(8,128)}, s32[]{:T(128)}, /*index=5*/s32[]{:T(128)}) %tuple.79), condition=%wide.region_1.2_spmd.clone, body=%wide.region_0.1_spmd.clone.sunk | while | flops 393220 | bytes 1572965 | solution.py:24
  158.5 1.3 add_select_fusion.4
  159.8 1.2 add_select_fusion.4
  161.0 1.2 add_select_fusion.4
  162.3 1.2 add_select_fusion.4
  163.5 1.2 add_select_fusion.4
  164.8 1.2 add_select_fusion.4
  166.0 1.2 add_select_fusion.4
  167.3 1.2 add_select_fusion.4
  168.5 1.2 add_select_fusion.4
  169.8 1.2 add_select_fusion.4
  171.0 1.2 add_select_fusion.4
  172.3 1.2 add_select_fusion.4
  173.5 1.2 add_select_fusion.4
  174.8 1.2 add_select_fusion.4
  176.0 1.2 add_select_fusion.4
  177.3 1.2 add_select_fusion.4
  178.5 1.2 add_select_fusion.4
  179.8 1.2 add_select_fusion.4
  189.8 1.2 add_select_fusion.4
  197.3 4.1 fusion.2
  201.4 3.0 copy.43
  204.4 2.6 multiply_reduce_fusion
  207.0 13.0 %all-reduce = (f32[512]{0:T(512)S(1)}, f32[512]{0:T(512)S(1)}) all-reduce(f32[512]{0:T(512)S(1)} %get-tuple-element.228, f32[512]{0:T(512)S(1)} %multiply_reduce_fusion), channel_id=1, replica_groups=mesh['ctx'=32,'tp'=8] {'tp'}, use_global_device_ids=true, to_apply=%region_3.4 | all-reduce | flops 1024 | bytes 8192 | tf_op jit(solution)/shard_map/psum | solution.py:59
  220.0 4.9 %multiply_convert_fusion = (bf16[512,1024]{1,0:T(8,128)(2,1)}, bf16[512,1024]{1,0:T(8,128)(2,1)}, bf16[512,1024]{1,0:T(8,128)(2,1)}) fusion(bf16[512,1024]{1,0:T(8,128)(2,1)S(1)} %copy-done.14, f32[512,1024]{1,0:T(8,128)} %copy.43, f32[1024]{0:T(1024)S(1)} %copy-done.15, f32[512]{0:T(512)S(1)} %get-tuple-element.227, bf16[512,1024]{1,0:T(8,128)(2,1)} %param.13, ...), kind=kLoop, calls=%fused_computation.11 | loop fusion | flops 10485760 | bytes 7348224 | tf_op jit(solution)/shard_map/convert_element_type | solution.py:66
  224.8 1.5 copy.63
  227.9 2.7 select_convert_fusion
  230.6 1.5 fusion.27
  232.6 2.1 fusion.1
  234.7 2.3 copy.58
  236.9 4.5 %fusion.28 = f32[8,128,512]{2,1,0:T(8,128)} fusion(bf16[512,8,128]{0,2,1:T(8,128)(2,1)S(1)} %bitcast.119, bf16[8,512,512]{2,1,0:T(8,128)(2,1)} %copy-done.1), kind=kOutput, calls=%fused_computation.49 | convolution fusion | flops 536870912 | bytes 7340032 | tf_op jit(solution)/shard_map/nhbc,nbhf->nchf/dot_general | solution.py:86
  241.4 123.1 %all-gather.7.cloned.1.call-done = f32[256,128,128]{2,1,0:T(8,128)} async-done(((f32[8,128,128]{2,1,0:T(8,128)}), f32[256,128,128]{2,1,0:T(8,128)}) %all-gather.7.cloned.1.call-update) | async-done | bytes 16777232 | tf_op jit(solution)/shard_map/all_gather | solution.py:14
  364.5 11.7 %rev.3 = f32[32,8,128,128]{3,2,1,0:T(8,128)} reverse(f32[32,8,128,128]{3,2,1,0:T(8,128)} %bitcast.120), dimensions={0} | reverse | bytes 33554432 | tf_op jit(solution)/shard_map/rev | solution.py:16
  376.2 38.9 %while.29 = (s32[]{:T(128)}, f32[8,128,128]{2,1,0:T(8,128)S(1)}, s32[]{:T(128)}, f32[32,8,128,128]{3,2,1,0:T(8,128)}, s32[]{:T(128)}, /*index=5*/s32[]{:T(128)}) while((s32[]{:T(128)}, f32[8,128,128]{2,1,0:T(8,128)S(1)}, s32[]{:T(128)}, f32[32,8,128,128]{3,2,1,0:T(8,128)}, s32[]{:T(128)}, /*index=5*/s32[]{:T(128)}) %tuple.72), condition=%wide.region_7.8_spmd.clone, body=%wide.region_6.7_spmd.clone.sunk | while | flops 393220 | bytes 1572965 | solution.py:24
  376.2 1.3 add_select_fusion.5
  391.4 1.2 add_select_fusion.5
  392.6 1.2 add_select_fusion.5
  416.2 3.6 fusion.6
  420.9 1.3 copy.60
  422.3 3.7 fusion
  425.9 1.3 copy.59
  (83 shorter events, 53.4 us)
Async XLA Ops:
  7.2 7.3 %copy-start = (bf16[512,1024]{1,0:T(8,128)(2,1)S(1)}, bf16[512,1024]{1,0:T(8,128)(2,1)}, u32[]{:S(2)}) copy-start(bf16[512,1024]{1,0:T(8,128)(2,1)} %param.10) | copy-start | bytes 3145732
  7.2 151.3 %all-gather.5.cloned.1.call-start = ((), (), s32[]{:S(2)}) async-start(), calls=%async_computation | async-start | bytes 17301504 | tf_op jit(solution)/shard_map/all_gather | solution.py:14
  11.4 5.7 %copy-start.3 = (bf16[512,8,128]{0,2,1:T(8,128)(2,1)}, bf16[512,8,128]{0,2,1:T(8,128)(2,1)S(1)}, u32[]{:S(2)}) copy-start(bf16[512,8,128]{0,2,1:T(8,128)(2,1)S(1)} %copy.39) | copy-start | bytes 3145732
  14.3 350.2 %all-gather.7.cloned.1.call-start = ((), (), s32[]{:S(2)}) async-start(), calls=%async_computation.1 | async-start | bytes 17301504 | tf_op jit(solution)/shard_map/all_gather | solution.py:14
  14.5 4.7 %copy-start.5 = (bf16[512,1024]{1,0:T(8,128)(2,1)S(1)}, bf16[512,1024]{1,0:T(8,128)(2,1)}, u32[]{:S(2)}) copy-start(bf16[512,1024]{1,0:T(8,128)(2,1)} %param.12) | copy-start | bytes 3145732
  17.1 2.1 copy-start.1
  158.5 38.8 %copy-start.7 = (f32[8,128,128]{2,1,0:T(8,128)S(1)}, f32[8,128,128]{2,1,0:T(8,128)}, u32[]{:S(2)}) copy-start(f32[8,128,128]{2,1,0:T(8,128)} %fusion.9) | copy-start | bytes 1572868
  201.4 3.0 copy-start.14
  201.4 3.0 copy-start.15
  226.8 1.0 copy-start.10
  227.8 2.7 copy-start.4
  230.6 2.0 copy-start.2
  230.6 2.0 copy-start.8
  376.2 39.9 %copy-start.6 = (bf16[512,1024]{1,0:T(8,128)(2,1)S(1)}, bf16[512,1024]{1,0:T(8,128)(2,1)}, u32[]{:S(2)}) copy-start(bf16[512,1024]{1,0:T(8,128)(2,1)} %param.12) | copy-start | bytes 3145732
  376.2 39.9 %copy-start.11 = (f32[8,128,128]{1,2,0:T(8,128)S(1)}, f32[8,128,128]{1,2,0:T(8,128)}, u32[]{:S(2)}) copy-start(f32[8,128,128]{1,2,0:T(8,128)} %copy-done.10) | copy-start | bytes 1572868
  416.1 3.6 copy-start.9
  416.1 3.6 copy-start.12
  416.2 3.6 copy-start.13
Sparse Core Ops, SparseCore 0:
  14.4 143.9 all-gather.4
  228.0 136.5 all-gather.6
where the time goes:
time: 437 us; the launch traced here: 434 us
  waiting for transfers between devices  260 us (59%)
  other arithmetic  83.8 us (19%)
  matrix products  32 us (7%)
  local copies, waits for them, and re-layouts  29.9 us (7%)
  between operations  14.3 us (3%)
  blocking collectives  13 us (3%)
    all_gather x2, waiting for transfers between devices, carried_in(): pieces = lax.all_gather(value, axis)  260 us
    select_n x62, other arithmetic, turn(): return jnp.where(position < mine, longer, running)  76.2 us
    psum x1, blocking collectives, local(): square_total = lax.psum(own_square, 'tp')  13 us
    rev x1, local copies, waits for them, and re-layouts, carried_in(): pieces = pieces[::-1]  11.7 us
    unnamed x36, local copies, waits for them, and re-layouts  10.1 us
  transfers between devices with their start and end apart: 2, of which 2 were waited for; matrix products, arithmetic and copies ran while one was open for 4% of the time, Pallas kernels for 0%

commit v1 on v0

--- a/solution.py
+++ b/solution.py
@@ -56,7 +56,8 @@
     dy_full = out_grad.astype(jnp.float32)
     dn = dy_full * gain * sig
     own_square = jnp.sum(mixed * mixed, axis=1)
-    square_total = lax.psum(own_square, "tp")
+    parts = lax.all_gather(own_square, "tp")
+    square_total = jnp.sum(parts, axis=0)
     inv_rms = lax.rsqrt(square_total / D + EPS)[:, None]
     normed = mixed * inv_rms
     output = (normed * gain * sig).astype(jnp.bfloat16)

time: 437 us -> 452 us (1.034)
  blocking collectives: 13 us -> 26.4 us
    all_gather x0 -> x1, blocking collectives: none -> 13.6 us  [local(): parts = lax.all_gather(own_square, 'tp')]
    unnamed x36 -> x38, local copies, waits for them, and re-layouts: 10.1 us -> 12.2 us
where the time goes in v1:
time: 452 us; the launch traced here: 449 us
  waiting for transfers between devices  259 us (57%)
  other arithmetic  83.8 us (19%)
  local copies, waits for them, and re-layouts  32 us (7%)
  matrix products  31.6 us (7%)
  blocking collectives  26.4 us (6%)
  between operations  14.3 us (3%)
    all_gather x2, waiting for transfers between devices, carried_in(): pieces = lax.all_gather(value, axis)  259 us
    select_n x62, other arithmetic, turn(): return jnp.where(position < mine, longer, running)  76.2 us
    all_gather x1, blocking collectives, local(): parts = lax.all_gather(own_square, 'tp')  13.6 us
    psum x1, blocking collectives, local(): cross_total = lax.psum(jnp.sum(dn * mixed, axis=1), 'tp')  12.8 us
    unnamed x38, local copies, waits for them, and re-layouts  12.2 us
    rev x1, local copies, waits for them, and re-layouts, carried_in(): pieces = pieces[::-1]  11.7 us
  transfers between devices with their start and end apart: 2, of which 2 were waited for; matrix products, arithmetic and copies ran while one was open for 4% of the time, Pallas kernels for 0%

profile of v1, /device:TPU:1, one launch (start us, length us, event | category | flops | bytes accessed | tf_op | source)
XLA Modules:
  0.0 449.0 jit_solution(16661713911482261704)
XLA Ops:
  7.2 2.6 copy.67
  9.8 1.6 copy.39
  11.5 1.3 fusion.9
  13.0 2.5 select_convert_fusion.1
  15.5 2.1 copy-done.1
  17.6 2.9 fusion.4
  20.4 136.5 %all-gather.7.cloned.1.call-done = f32[256,128,128]{2,1,0:T(8,128)} async-done(((f32[8,128,128]{2,1,0:T(8,128)}), f32[256,128,128]{2,1,0:T(8,128)}) %all-gather.7.cloned.1.call-update) | async-done | bytes 16777232 | tf_op jit(solution)/shard_map/all_gather | solution.py:14
  156.9 38.8 %while.28 = (s32[]{:T(128)}, f32[8,128,128]{2,1,0:T(8,128)S(1)}, s32[]{:T(128)}, f32[32,8,128,128]{3,2,1,0:T(8,128)}, s32[]{:T(128)}, /*index=5*/s32[]{:T(128)}) while((s32[]{:T(128)}, f32[8,128,128]{2,1,0:T(8,128)S(1)}, s32[]{:T(128)}, f32[32,8,128,128]{3,2,1,0:T(8,128)}, s32[]{:T(128)}, /*index=5*/s32[]{:T(128)}) %tuple.79), condition=%wide.region_1.2_spmd.clone, body=%wide.region_0.1_spmd.clone.sunk | while | flops 393220 | bytes 1572965 | solution.py:24
  156.9 1.3 add_select_fusion.4
  158.2 1.2 add_select_fusion.4
  159.5 1.2 add_select_fusion.4
  160.7 1.2 add_select_fusion.4
  162.0 1.2 add_select_fusion.4
  163.2 1.2 add_select_fusion.4
  164.5 1.2 add_select_fusion.4
  165.8 1.2 add_select_fusion.4
  167.0 1.2 add_select_fusion.4
  168.3 1.2 add_select_fusion.4
  169.5 1.2 add_select_fusion.4
  170.8 1.2 add_select_fusion.4
  172.0 1.2 add_select_fusion.4
  173.3 1.2 add_select_fusion.4
  174.5 1.2 add_select_fusion.4
  175.8 1.2 add_select_fusion.4
  182.0 1.2 add_select_fusion.4
  195.8 4.1 fusion.2
  199.8 3.0 copy.43
  202.9 2.6 multiply_reduce_fusion
  205.5 12.8 %psum.7 = f32[512]{0:T(512)S(1)} all-reduce(f32[512]{0:T(512)S(1)} %multiply_reduce_fusion), channel_id=1, replica_groups=mesh['ctx'=32,'tp'=8] {'tp'}, use_global_device_ids=true, to_apply=%region_5.6 | all-reduce | flops 512 | bytes 4096 | tf_op jit(solution)/shard_map/psum | solution.py:64
  218.3 13.6 %all-gather.3 = f32[8,1,512]{2,1,0:T(1,128)S(1)} all-gather(f32[1,1,512]{2,1,0:T(1,128)S(1)} %bitcast.129), channel_id=3, replica_groups=mesh['ctx'=32,'tp'=8] {'tp'}, dimensions={0}, use_global_device_ids=true | all-gather | bytes 18432 | tf_op jit(solution)/shard_map/all_gather | solution.py:59
  231.9 4.9 %multiply_convert_fusion = (bf16[512,1024]{1,0:T(8,128)(2,1)}, bf16[512,1024]{1,0:T(8,128)(2,1)}, bf16[512,1024]{1,0:T(8,128)(2,1)}) fusion(bf16[512,1024]{1,0:T(8,128)(2,1)S(1)} %copy-done.15, f32[512,1024]{1,0:T(8,128)} %copy.43, f32[1024]{0:T(1024)S(1)} %copy-done.16, f32[512]{0:T(512)S(1)} %get-tuple-element.225, bf16[512,1024]{1,0:T(8,128)(2,1)} %param.13, ...), kind=kLoop, calls=%fused_computation.11 | loop fusion | flops 10485760 | bytes 7348224 | tf_op jit(solution)/shard_map/convert_element_type | solution.py:67
  236.8 1.5 copy.63
  239.8 2.7 select_convert_fusion
  242.6 1.5 fusion.27
  244.5 2.1 fusion.1
  246.6 2.3 copy.58
  248.9 4.4 fusion.28
  253.3 122.8 %all-gather.9.cloned.1.call-done = f32[256,128,128]{2,1,0:T(8,128)} async-done(((f32[8,128,128]{2,1,0:T(8,128)}), f32[256,128,128]{2,1,0:T(8,128)}) %all-gather.9.cloned.1.call-update) | async-done | bytes 16777232 | tf_op jit(solution)/shard_map/all_gather | solution.py:14
  376.1 11.7 %rev.3 = f32[32,8,128,128]{3,2,1,0:T(8,128)} reverse(f32[32,8,128,128]{3,2,1,0:T(8,128)} %bitcast.121), dimensions={0} | reverse | bytes 33554432 | tf_op jit(solution)/shard_map/rev | solution.py:16
  387.8 38.9 %while.29 = (s32[]{:T(128)}, f32[8,128,128]{2,1,0:T(8,128)S(1)}, s32[]{:T(128)}, f32[32,8,128,128]{3,2,1,0:T(8,128)}, s32[]{:T(128)}, /*index=5*/s32[]{:T(128)}) while((s32[]{:T(128)}, f32[8,128,128]{2,1,0:T(8,128)S(1)}, s32[]{:T(128)}, f32[32,8,128,128]{3,2,1,0:T(8,128)}, s32[]{:T(128)}, /*index=5*/s32[]{:T(128)}) %tuple.72), condition=%wide.region_7.8_spmd.clone, body=%wide.region_6.7_spmd.clone.sunk | while | flops 393220 | bytes 1572965 | solution.py:24
  387.8 1.3 add_select_fusion.5
  406.7 1.2 add_select_fusion.5
  408.0 1.2 add_select_fusion.5
  427.8 3.6 fusion.6
  431.4 2.1 add_convert_fusion
  433.5 2.4 copy.60
  435.9 4.0 fusion
  439.9 2.3 copy.59
  (87 shorter events, 54.8 us)
Async XLA Ops:
  7.2 5.8 %copy-start = (bf16[512,1024]{1,0:T(8,128)(2,1)S(1)}, bf16[512,1024]{1,0:T(8,128)(2,1)}, u32[]{:S(2)}) copy-start(bf16[512,1024]{1,0:T(8,128)(2,1)} %param.10) | copy-start | bytes 3145732
  7.2 149.8 %all-gather.7.cloned.1.call-start = ((), (), s32[]{:S(2)}) async-start(), calls=%async_computation | async-start | bytes 17301504 | tf_op jit(solution)/shard_map/all_gather | solution.py:14
  7.2 4.3 copy-start.5
  11.5 1.3 copy-start.3
  12.8 363.3 %all-gather.9.cloned.1.call-start = ((), (), s32[]{:S(2)}) async-start(), calls=%async_computation.1 | async-start | bytes 17301504 | tf_op jit(solution)/shard_map/all_gather | solution.py:14
  15.5 2.1 copy-start.1
  156.9 38.8 %copy-start.7 = (f32[8,128,128]{2,1,0:T(8,128)S(1)}, f32[8,128,128]{2,1,0:T(8,128)}, u32[]{:S(2)}) copy-start(f32[8,128,128]{2,1,0:T(8,128)} %fusion.9) | copy-start | bytes 1572868
  199.8 3.0 copy-start.15
  199.8 3.0 copy-start.16
  238.7 1.0 copy-start.10
  239.8 2.7 copy-start.4
  242.5 2.0 copy-start.2
  242.5 2.0 copy-start.8
  387.8 39.9 %copy-start.6 = (bf16[512,1024]{1,0:T(8,128)(2,1)S(1)}, bf16[512,1024]{1,0:T(8,128)(2,1)}, u32[]{:S(2)}) copy-start(bf16[512,1024]{1,0:T(8,128)(2,1)} %param.12) | copy-start | bytes 3145732
  387.8 39.9 %copy-start.11 = (f32[8,128,128]{1,2,0:T(8,128)S(1)}, f32[8,128,128]{1,2,0:T(8,128)}, u32[]{:S(2)}) copy-start(f32[8,128,128]{1,2,0:T(8,128)} %copy-done.10) | copy-start | bytes 1572868
  427.7 3.6 copy-start.9
  427.8 3.6 copy-start.13
  427.8 3.6 copy-start.14
  433.5 2.4 copy-start.12
Sparse Core Ops, SparseCore 0:
  12.9 143.9 all-gather.6
  239.9 136.1 all-gather.8
